TPU v7x, 32 devices: a whole 2x2x4 slice. The times are simulated.
32 devices in a mesh: req: 4 (over y, core), voc: 8 (over z, x).
Axes of the slice: x: 2, y: 2, z: 4, core: 2. Of those that a mesh axis runs over, the one named last changes fastest.
Arguments:
- hidden: bfloat16 [4096, 1536], P(('req', 'voc')), may hold values from -64 to 64
- norm_gain: float32 [1536], replicated, may hold values from 0.1 to 1.9
- head: bfloat16 [1536, 49152], P(None, 'voc'), may hold values from -8 to 8
- targets: int32 [4096], P(('req', 'voc')), may hold values from 0 to 49151
- bounds: int32 [32, 2], P(('req', 'voc')), may hold values from 0 to 128, as said below
Outputs:
- logprob: float32 [4096], P(('req', 'voc'))
- entropy: float32 [4096], P(('req', 'voc'))
- target_logit: float32 [4096], P(('req', 'voc'))
- mean_entropy: float32 [1], replicated
Inputs may be any that keep to these rules, and one draw needn't show every extreme that they name: bounds[d] = (lo, hi): slots lo to hi - 1 of device d hold live response rows; 1 <= hi - lo <= 96, lo <= 32; some device has hi - lo = 96 and hi = 128, some has lo = 0.
All inputs are finite; a program needn't handle non-finite values.
Results may differ from a plain program's by a relative error of at most 0.00075.
The roundings to bfloat16 on the way count: a program that leaves them out, or rounds other values in their place, can miss the bound.
Values may be sent and summed in bfloat16 or wider, within the bound.
A program may use at most 64 MiB of HBM per device.

v0:
```python
import jax
import jax.numpy as jnp
from jax import lax
from jax.sharding import PartitionSpec as P


def joined(part, axis, combine):
    gathered = jax.tree.map(lambda a: lax.all_gather(a, axis), part)

    def take(source):
        return jax.tree.map(lambda a: lax.dynamic_index_in_dim(a, source, 0, False), gathered)

    return lax.fori_loop(
        1, lax.axis_size(axis), lambda source, state: combine(state, take(source)), take(0)
    )


def pick_block(count):
    size = min(count, 512)
    while count % size:
        size -= 1
    return size


def combine_stats(first, second):
    top = jnp.maximum(first[0], second[0])
    weight_a = jnp.exp(first[0] - top)
    weight_b = jnp.exp(second[0] - top)
    return (
        top,
        first[1] * weight_a + second[1] * weight_b,
        first[2] * weight_a + second[2] * weight_b,
        first[3] + second[3],
    )


def shard_stats(gathered, local_ids, head):
    count = gathered.shape[0]
    width = gathered.shape[1]
    block = pick_block(count)
    columns = jnp.arange(head.shape[1], dtype=jnp.int32)

    def one_block(pair):
        rows_in, ids = pair
        logits = jnp.dot(rows_in, head, preferred_element_type=jnp.float32)
        top = jnp.max(logits, axis=-1)
        expo = jnp.exp(logits - top[:, None])
        total = jnp.sum(expo, axis=-1)
        weighted = jnp.sum(expo * logits, axis=-1)
        picked = jnp.sum(jnp.where(columns[None, :] == ids[:, None], logits, 0.0), axis=-1)
        return (top, total, weighted, picked)

    outputs = lax.map(
        one_block,
        (gathered.reshape(count // block, block, width), local_ids.reshape(count // block, block)),
    )
    return tuple((a.reshape(count) for a in outputs))


def shards(hidden, norm_gain, head, targets, bounds):
    slots = hidden.shape[0]
    shard_width = head.shape[1]
    position = lax.axis_index("voc")
    values = hidden.astype(jnp.float32)
    meansq = jnp.mean(values * values, axis=-1, keepdims=True)
    normed = (values * lax.rsqrt(meansq + 1e-05) * norm_gain).astype(jnp.bfloat16)
    start = bounds[0, 0]
    finish = bounds[0, 1]
    gathered, gathered_ids = (
        lax.all_gather(normed, "voc", axis=0, tiled=True),
        lax.all_gather(targets, "voc", axis=0, tiled=True),
    )
    local_ids = gathered_ids - position * shard_width
    stats = shard_stats(gathered, local_ids, head)
    merged = joined(stats, "voc", combine_stats)
    top, total, weighted, picked = [
        lax.dynamic_slice_in_dim(a, position * slots, slots, 0) for a in merged
    ]
    lse = top + jnp.log(total)
    row_entropy = lse - weighted / total
    row_logprob = picked - lse
    slot_index = jnp.arange(slots, dtype=jnp.int32)
    live = (slot_index >= start) & (slot_index < finish)
    zero = jnp.zeros((slots,), jnp.float32)
    entropy = jnp.where(live, row_entropy, zero)
    logprob = jnp.where(live, row_logprob, zero)
    target_logit = jnp.where(live, picked, zero)
    ent_sum, live_count = lax.psum(
        (jnp.sum(entropy), jnp.sum(live.astype(jnp.float32))), ("req", "voc")
    )
    mean_entropy = (ent_sum / live_count).reshape(1)
    return (logprob, entropy, target_logit, mean_entropy)


def solution(mesh):
    placed = (
        P(("req", "voc"), None),
        P(),
        P(None, "voc"),
        P(("req", "voc")),
        P(("req", "voc"), None),
    )
    return jax.shard_map(
        shards,
        mesh=mesh,
        in_specs=placed,
        out_specs=(P(("req", "voc")), P(("req", "voc")), P(("req", "voc")), P()),
        check_vma=False,
    )
```

profile of v0, /device:TPU:0, one launch (start us, length us, event | category | flops | bytes accessed | tf_op | source)
XLA Modules:
  0.0 281.6 jit_solution(873592637509625194)
XLA Ops:
  7.2 0.0 all-gather.7.cloned.1.call-start
  7.2 1.2 fusion.7
  8.4 1.9 fusion.9
  10.3 0.0 all-gather.7.cloned.1.call-update
  10.4 22.3 %all-gather = s32[8,1,128]{2,1,0:T(1,128)S(1)} all-gather(s32[1,1,128]{2,1,0:T(1,128)} %bitcast.76), channel_id=1, replica_groups=mesh['req'=4,'voc'=8] {'voc'}, dimensions={0}, use_global_device_ids=true | all-gather | bytes 4608 | tf_op jit(solution)/shard_map/all_gather | solution.py:71
  32.7 1.3 fusion.12
  34.0 1.9 convert_reduce_fusion
  35.9 37.6 %all-gather.7.cloned.1.call-done = bf16[1024,1536]{1,0:T(8,128)(2,1)} async-done(((bf16[128,1536]{1,0:T(8,128)(2,1)}), bf16[1024,1536]{1,0:T(8,128)(2,1)}) %all-gather.7.cloned.1.call-update) | async-done | bytes 3145744 | tf_op jit(solution)/shard_map/all_gather | solution.py:70
  73.6 37.3 %while.39 = (s32[]{:T(128)}, f32[2,512]{1,0:T(2,128)S(1)}, f32[2,512]{1,0:T(2,128)S(1)}, f32[2,512]{1,0:T(2,128)S(1)}, f32[2,512]{1,0:T(2,128)S(1)}, /*index=5*/...) while((s32[]{:T(128)}, f32[2,512]{1,0:T(2,128)S(1)}, ...), condition=%wide.region_6.7_spmd.clone, body=%wide.region_1.6_spmd.clone.sunk | while | flops 9688840192 | bytes 45646456 | solution.py:53
  73.6 13.8 %fusion.17 = (f32[512]{0:T(512)S(1)}, f32[512,6144]{1,0:T(8,128)S(1)}) fusion(bf16[1536,6144]{1,0:T(8,128)(2,1)} %get-tuple-element.510, bf16[2,512,1536]{2,1,0:T(8,128)(2,1)} %get-tuple-element.509, s32[]{:T(128)} %get-tuple-element.494), kind=kOutput, calls=%fused_computation.37.clone.1 | convolution fusion | flops 9666822144 | bytes 33032704 | tf_op jit(solution)/shard_map/while/body/eval_jaxpr/dot_general | solution.py:45
  87.3 4.7 %multiply_reduce_fusion.2 = (f32[512]{0:T(512)S(1)}, f32[512]{0:T(512)S(1)}, f32[512]{0:T(512)S(1)}) fusion(f32[512,6144]{1,0:T(8,128)S(1)} %get-tuple-element.480, f32[512]{0:T(512)S(1)} %get-tuple-element.479, s32[512]{0:T(512)S(1)} %bitcast.68), kind=kLoop, calls=%fused_computation.11.clone.1 | loop fusion | flops 22018560 | bytes 12593152 | tf_op jit(solution)/shard_map/while/body/eval_jaxpr/reduce_sum | solution.py:49
  92.2 13.8 %fusion.17 = (f32[512]{0:T(512)S(1)}, f32[512,6144]{1,0:T(8,128)S(1)}) fusion(bf16[1536,6144]{1,0:T(8,128)(2,1)} %get-tuple-element.510, bf16[2,512,1536]{2,1,0:T(8,128)(2,1)} %get-tuple-element.509, s32[]{:T(128)} %get-tuple-element.494), kind=kOutput, calls=%fused_computation.37.clone.1 | convolution fusion | flops 9666822144 | bytes 33032704 | tf_op jit(solution)/shard_map/while/body/eval_jaxpr/dot_general | solution.py:45
  106.0 4.7 %multiply_reduce_fusion.2 = (f32[512]{0:T(512)S(1)}, f32[512]{0:T(512)S(1)}, f32[512]{0:T(512)S(1)}) fusion(f32[512,6144]{1,0:T(8,128)S(1)} %get-tuple-element.480, f32[512]{0:T(512)S(1)} %get-tuple-element.479, s32[512]{0:T(512)S(1)} %bitcast.68), kind=kLoop, calls=%fused_computation.11.clone.1 | loop fusion | flops 22018560 | bytes 12593152 | tf_op jit(solution)/shard_map/while/body/eval_jaxpr/reduce_sum | solution.py:49
  110.9 30.4 %all-gather.3 = f32[8,1,1024]{2,1,0:T(1,128)S(1)} all-gather(f32[1,1,1024]{2,1,0:T(1,128)S(1)} %reshape.39), channel_id=1, replica_groups=mesh['req'=4,'voc'=8] {'voc'}, dimensions={0}, use_global_device_ids=true | all-gather | bytes 36864 | tf_op jit(solution)/shard_map/all_gather | solution.py:8
  141.4 30.4 %all-gather.4 = f32[8,1,1024]{2,1,0:T(1,128)S(1)} all-gather(f32[1,1,1024]{2,1,0:T(1,128)S(1)} %reshape.41), channel_id=1, replica_groups=mesh['req'=4,'voc'=8] {'voc'}, dimensions={0}, use_global_device_ids=true | all-gather | bytes 36864 | tf_op jit(solution)/shard_map/all_gather | solution.py:8
  171.8 30.4 %all-gather.1 = f32[8,1,1024]{2,1,0:T(1,128)S(1)} all-gather(f32[1,1,1024]{2,1,0:T(1,128)S(1)} %reshape.35), channel_id=1, replica_groups=mesh['req'=4,'voc'=8] {'voc'}, dimensions={0}, use_global_device_ids=true | all-gather | bytes 36864 | tf_op jit(solution)/shard_map/all_gather | solution.py:8
  202.3 30.4 %all-gather.2 = f32[8,1,1024]{2,1,0:T(1,128)S(1)} all-gather(f32[1,1,1024]{2,1,0:T(1,128)S(1)} %reshape.37), channel_id=1, replica_groups=mesh['req'=4,'voc'=8] {'voc'}, dimensions={0}, use_global_device_ids=true | all-gather | bytes 36864 | tf_op jit(solution)/shard_map/all_gather | solution.py:8
  232.7 0.8 while.38
  233.5 1.2 fusion.10
  234.8 37.5 %all-reduce = (f32[]{:T(128)}, f32[]{:T(128)}) all-reduce(f32[]{:T(128)} %get-tuple-element.346, f32[]{:T(128)} %get-tuple-element.344), channel_id=1, replica_groups=mesh['req'=4,'voc'=8] {'req','voc'}, use_global_device_ids=true, to_apply=%region_10.11 | all-reduce | flops 2 | bytes 16 | tf_op jit(solution)/shard_map/psum | solution.py:88
  (71 shorter events, 0.9 us)
Async XLA Ops:
  7.2 66.4 %all-gather.7.cloned.1.call-start = ((), (), s32[]{:S(2)}) async-start(), calls=%async_computation | async-start | bytes 3538944 | tf_op jit(solution)/shard_map/all_gather | solution.py:70
Sparse Core Ops, SparseCore 0:
  10.4 63.0 all-gather.6
where the time goes:
time: 283 us; the launch traced here: 282 us
  blocking collectives  181 us (64%)
  waiting for transfers between devices  37.6 us (13%)
  matrix products  27.5 us (10%)
  between operations  16.7 us (6%)
  other arithmetic  15.8 us (6%)
    all_gather x4, blocking collectives, joined(): gathered = jax.tree.map(lambda a: lax.all_gather(a, axis), part)  122 us
    all_gather x1, waiting for transfers between devices, shards(): lax.all_gather(normed, 'voc', axis=0, tiled=True)  37.6 us
    psum x1, blocking collectives, shards(): lax.psum((jnp.sum(entropy), jnp.sum(live.astype(jnp.float32))), ('req', '...  37.5 us
    dot_general x2, matrix products, one_block(): logits = jnp.dot(rows_in, head, preferred_element_type=jnp.float32)  27.5 us
    all_gather x1, blocking collectives, shards(): lax.all_gather(targets, 'voc', axis=0, tiled=True)  22.3 us
    reduce_sum x2, other arithmetic, one_block(): weighted = jnp.sum(expo * logits, axis=-1)  9.39 us
  transfers between devices with their start and end apart: 1, of which 1 were waited for; matrix products, arithmetic and copies ran while one was open for 1% of the time, Pallas kernels for 0%

commit v1 on v0

v1 whole, which is shorter than its diff:
```python
import functools

import jax
import jax.numpy as jnp
from jax import lax
from jax.experimental import pallas as pl
from jax.experimental.pallas import tpu as pltpu
from jax.sharding import PartitionSpec as P

LIVE = 96
SIDE = 2
LANES = 128
CHUNK = 768
LOW = -1e30


def kernel(
    nreq, nvoc, bounds, hidden, gain, targets, head, logprob, entropy, picked_out, mean,
    rows, weights, first, second, top, total, weighted, picked, group,
    meta, stats, stats_out, ent, ent_sum,
    head_sem, rows_rx, down_tx, up_tx, side_tx, meta_rx, meta_tx, stats_rx, stats_tx,
    ent_rx, ent_tx, sum_rx, sum_tx,
):
    nz = nvoc // SIDE
    req = lax.axis_index("req")
    me = lax.axis_index("voc")
    x = lax.rem(me, SIDE)
    z = me // SIDE
    partner = z * SIDE + (SIDE - 1 - x)
    slots = hidden.shape[0]
    width = head.shape[1]
    chunks = width // CHUNK
    cells = CHUNK // LANES

    def at(place, side):
        return place * SIDE + side

    def load_head(c):
        return pltpu.make_async_copy(
            head.at[:, pl.ds(pl.multiple_of(c * CHUNK, CHUNK), CHUNK)], weights.at[c], head_sem.at[c]
        )

    barrier = pltpu.get_barrier_semaphore()
    for i in range(1, nvoc):
        pl.semaphore_signal(barrier, inc=1, device_id={"voc": lax.rem(me + i, nvoc)})
    for i in range(1, nreq):
        pl.semaphore_signal(barrier, inc=1, device_id={"req": lax.rem(req + i, nreq)})

    for c in range(chunks):
        load_head(c).start()

    lo = bounds[0, 0]
    hi = bounds[0, 1]
    values = hidden[...].astype(jnp.float32)
    meansq = jnp.mean(values * values, axis=-1, keepdims=True)
    normed = (values * lax.rsqrt(meansq + 1e-05) * gain[...]).astype(jnp.bfloat16)
    slot = lax.broadcasted_iota(jnp.int32, (LIVE, slots), 1)
    order = lax.broadcasted_iota(jnp.int32, (LIVE, slots), 0)
    window = jnp.where(slot == order + lo, 1.0, 0.0).astype(jnp.bfloat16)
    rows[me] = jnp.dot(window, normed, preferred_element_type=jnp.float32).astype(jnp.bfloat16)
    tile_row = lax.broadcasted_iota(jnp.int32, (8, slots), 0)
    meta[me] = jnp.where(tile_row == 0, jnp.broadcast_to(targets[...], (8, slots)), lo)

    pl.semaphore_wait(barrier, nvoc - 1 + nreq - 1)

    def send_rows(source, target, sem):
        return pltpu.make_async_remote_copy(
            src_ref=rows.at[source], dst_ref=rows.at[source], send_sem=sem,
            recv_sem=rows_rx.at[source], device_id={"voc": target},
        )

    def send_down(place):
        return send_rows(at(place, x), at(z - 1, x), down_tx.at[place])

    def send_up(place):
        return send_rows(at(place, x), at(z + 1, x), up_tx.at[place])

    def send_side(place):
        return send_rows(at(place, x), partner, side_tx.at[place])

    def send_meta(i):
        return pltpu.make_async_remote_copy(
            src_ref=meta.at[me], dst_ref=meta.at[me], send_sem=meta_tx.at[i],
            recv_sem=meta_rx.at[me], device_id={"voc": lax.rem(me + i, nvoc)},
        )

    @pl.when(z > 0)
    def _():
        send_down(z).start()

    @pl.when(z < nz - 1)
    def _():
        send_up(z).start()

    send_side(z).start()
    for i in range(1, nvoc):
        send_meta(i).start()

    def local_ids(block):
        ids = jnp.broadcast_to(meta[block, 0:1, :], (LIVE, slots))
        start = jnp.broadcast_to(meta[block, 1:2, :], (LIVE, slots))
        hit = slot == order + start
        id_column = jnp.sum(jnp.where(hit, ids, 0).astype(jnp.float32), axis=-1, keepdims=True)
        return id_column.astype(jnp.int32) - me * width, hit

    def prepare(blocks):
        for n, block in enumerate(blocks):
            ids, _ = local_ids(block)
            group[pl.ds(n * LIVE, LIVE), :] = jnp.broadcast_to(ids >> 7, (LIVE, LANES))
        size = len(blocks) * LIVE
        top[pl.ds(0, size), :] = jnp.full((size, LANES), LOW, jnp.float32)
        for state in (total, weighted, picked):
            state[pl.ds(0, size), :] = jnp.zeros((size, LANES), jnp.float32)

    def multiply(blocks, c, out):
        left = [rows[block] for block in blocks]
        left = left[0] if len(left) == 1 else jnp.concatenate(left, axis=0)
        out[pl.ds(0, len(blocks) * LIVE), :] = jnp.dot(
            left, weights[c], preferred_element_type=jnp.float32
        )

    def absorb(count, c, logits):
        for r in range(0, count * LIVE, 8):
            here = pl.ds(r, 8)
            part = [logits[here, pl.ds(j * LANES, LANES)] for j in range(cells)]
            old = top[here, :]
            new = functools.reduce(jnp.maximum, part, old)
            scale = jnp.exp(old - new)
            expo = [jnp.exp(v - new) for v in part]
            top[here, :] = new
            total[here, :] = total[here, :] * scale + functools.reduce(jnp.add, expo)
            weighted[here, :] = weighted[here, :] * scale + functools.reduce(
                jnp.add, [e * v for e, v in zip(expo, part)]
            )
            wanted = group[here, :]
            found = picked[here, :]
            for j, v in enumerate(part):
                found = jnp.where(wanted == c * cells + j, v, found)
            picked[here, :] = found

    def block_stats(n, block):
        here = pl.ds(n * LIVE, LIVE)
        ids, hit = local_ids(block)
        best = jnp.max(top[here, :], axis=-1, keepdims=True)
        scale = jnp.exp(top[here, :] - best)
        lane = lax.broadcasted_iota(jnp.int32, (LIVE, LANES), 1)
        columns = (
            best,
            jnp.sum(total[here, :] * scale, axis=-1, keepdims=True),
            jnp.sum(weighted[here, :] * scale, axis=-1, keepdims=True),
            jnp.sum(jnp.where(lane == (ids & 127), picked[here, :], 0.0), axis=-1, keepdims=True),
        )
        lines = [jnp.sum(jnp.where(hit, col, 0.0), axis=0, keepdims=True) for col in columns]
        return jnp.concatenate(lines + [jnp.zeros((4, slots), jnp.float32)], axis=0)

    def work(blocks, fresh):
        def ready(c):
            if fresh:
                load_head(c).wait()

        prepare(blocks)
        ready(0)
        multiply(blocks, 0, first)

        def body(i, carry):
            c = i * 2
            ready(c + 1)
            multiply(blocks, c + 1, second)
            absorb(len(blocks), c, first)
            ready(c + 2)
            multiply(blocks, c + 2, first)
            absorb(len(blocks), c + 1, second)
            return carry

        lax.fori_loop(0, chunks // 2 - 1, body, 0)
        ready(chunks - 1)
        multiply(blocks, chunks - 1, second)
        absorb(len(blocks), chunks - 2, first)
        absorb(len(blocks), chunks - 1, second)

    def send_stats(block):
        return pltpu.make_async_remote_copy(
            src_ref=stats_out.at[block], dst_ref=stats.at[me], send_sem=stats_tx.at[block],
            recv_sem=stats_rx.at[me], device_id={"voc": block},
        )

    def give(n, block):
        stats_out[block] = block_stats(n, block)
        send_stats(block).start()

    def wait_meta(block):
        pltpu.make_async_remote_copy(
            src_ref=meta.at[block], dst_ref=meta.at[block], send_sem=meta_tx.at[0],
            recv_sem=meta_rx.at[block], device_id={"voc": partner},
        ).wait_recv()

    def wait_rows(block):
        send_rows(block, partner, side_tx.at[0]).wait_recv()

    near = jnp.minimum(z, nz - 1 - z)
    far_side = jnp.where(z > nz - 1 - z, -1, 1)

    def line(i):
        close = i < 2 * near
        step = jnp.where(close, i // 2 + 1, i - near + 1)
        side = jnp.where(close, 2 * lax.rem(i, 2) - 1, far_side)
        return z + side * step

    work([me], True)
    stats[me] = block_stats(0, me)

    def tick(t, carry):
        @pl.when(z - t >= 0)
        def _():
            wait_rows(at(z - t, x))

            @pl.when(z < nz - 1)
            def _():
                send_up(z - t).start()

            send_side(z - t).start()

        @pl.when(z + t < nz)
        def _():
            wait_rows(at(z + t, x))

            @pl.when(z > 0)
            def _():
                send_down(z + t).start()

            send_side(z + t).start()

        across = at(jnp.where(t == 1, z, line(jnp.maximum(t - 2, 0))), SIDE - 1 - x)
        along = at(line(t - 1), x)
        wait_rows(across)
        wait_meta(across)
        wait_meta(along)
        work([across, along], False)
        give(0, across)
        give(1, along)
        return carry

    lax.fori_loop(1, nz, tick, 0)
    last = at(line(nz - 2), SIDE - 1 - x)
    wait_rows(last)
    wait_meta(last)
    work([last], False)
    give(0, last)

    for i in range(1, nvoc):
        source = lax.rem(me + i, nvoc)
        pltpu.make_async_remote_copy(
            src_ref=stats_out.at[source], dst_ref=stats.at[source], send_sem=stats_tx.at[source],
            recv_sem=stats_rx.at[source], device_id={"voc": source},
        ).wait_recv()
    tiles = [stats[i] for i in range(nvoc)]
    best = functools.reduce(jnp.maximum, [tile[0:1] for tile in tiles])
    scales = [jnp.exp(tile[0:1] - best) for tile in tiles]
    all_total = functools.reduce(jnp.add, [tile[1:2] * s for tile, s in zip(tiles, scales)])
    all_weighted = functools.reduce(jnp.add, [tile[2:3] * s for tile, s in zip(tiles, scales)])
    chosen = functools.reduce(jnp.add, [tile[3:4] for tile in tiles])
    place = lax.broadcasted_iota(jnp.int32, (1, slots), 1)
    live = (place >= lo) & (place < hi)
    lse = best + jnp.log(all_total)
    row_entropy = jnp.where(live, lse - all_weighted / all_total, 0.0)
    logprob[...] = jnp.where(live, chosen - lse, 0.0)
    entropy[...] = row_entropy
    picked_out[...] = jnp.where(live, chosen, 0.0)

    ent[me] = jnp.concatenate(
        [row_entropy, jnp.where(live, 1.0, 0.0), jnp.zeros((6, slots), jnp.float32)], axis=0
    )

    def send_ent(i):
        return pltpu.make_async_remote_copy(
            src_ref=ent.at[me], dst_ref=ent.at[me], send_sem=ent_tx.at[i],
            recv_sem=ent_rx.at[me], device_id={"voc": lax.rem(me + i, nvoc)},
        )

    def send_sum(i):
        return pltpu.make_async_remote_copy(
            src_ref=ent_sum.at[req], dst_ref=ent_sum.at[req], send_sem=sum_tx.at[i],
            recv_sem=sum_rx.at[req], device_id={"req": lax.rem(req + i, nreq)},
        )

    for i in range(1, nvoc):
        send_ent(i).start()
    for i in range(1, nvoc):
        source = lax.rem(me + i, nvoc)
        pltpu.make_async_remote_copy(
            src_ref=ent.at[source], dst_ref=ent.at[source], send_sem=ent_tx.at[i],
            recv_sem=ent_rx.at[source], device_id={"voc": source},
        ).wait_recv()
    ent_sum[req] = functools.reduce(jnp.add, [ent[i] for i in range(nvoc)])
    for i in range(1, nreq):
        send_sum(i).start()
    for i in range(1, nreq):
        source = lax.rem(req + i, nreq)
        pltpu.make_async_remote_copy(
            src_ref=ent_sum.at[source], dst_ref=ent_sum.at[source], send_sem=sum_tx.at[i],
            recv_sem=sum_rx.at[source], device_id={"req": source},
        ).wait_recv()
    summed = jnp.sum(functools.reduce(jnp.add, [ent_sum[i] for i in range(nreq)]), axis=-1, keepdims=True)
    mean[...] = summed[0:1] / summed[1:2]

    for place in range(nz):
        send_side(place).wait_send()

        @pl.when((z > 0) & (z <= place))
        def _():
            send_down(place).wait_send()

        @pl.when((z < nz - 1) & (z >= place))
        def _():
            send_up(place).wait_send()

    for i in range(1, nvoc):
        send_meta(i).wait_send()
        send_stats(lax.rem(me + i, nvoc)).wait_send()
        send_ent(i).wait_send()
    for i in range(1, nreq):
        send_sum(i).wait_send()


def shards(nreq, nvoc, hidden, norm_gain, head, targets, bounds):
    slots, depth = hidden.shape
    width = head.shape[1]
    nz = nvoc // SIDE
    chunks = width // CHUNK
    pair = 2 * LIVE
    vmem = pl.BlockSpec(memory_space=pltpu.VMEM)
    line = jax.ShapeDtypeStruct((1, slots), jnp.float32)
    dma = pltpu.SemaphoreType.DMA
    outs = pl.pallas_call(
        functools.partial(kernel, nreq, nvoc),
        out_shape=(line, line, line, jax.ShapeDtypeStruct((1, 1), jnp.float32)),
        in_specs=[
            pl.BlockSpec(memory_space=pltpu.SMEM), vmem, vmem, vmem, pl.BlockSpec(memory_space=pl.ANY),
        ],
        out_specs=(vmem, vmem, vmem, vmem),
        scratch_shapes=[
            pltpu.VMEM((nvoc, LIVE, depth), jnp.bfloat16),
            pltpu.VMEM((chunks, depth, CHUNK), jnp.bfloat16),
            pltpu.VMEM((pair, CHUNK), jnp.float32),
            pltpu.VMEM((pair, CHUNK), jnp.float32),
            pltpu.VMEM((pair, LANES), jnp.float32),
            pltpu.VMEM((pair, LANES), jnp.float32),
            pltpu.VMEM((pair, LANES), jnp.float32),
            pltpu.VMEM((pair, LANES), jnp.float32),
            pltpu.VMEM((pair, LANES), jnp.int32),
            pltpu.VMEM((nvoc, 8, slots), jnp.int32),
            pltpu.VMEM((nvoc, 8, slots), jnp.float32),
            pltpu.VMEM((nvoc, 8, slots), jnp.float32),
            pltpu.VMEM((nvoc, 8, slots), jnp.float32),
            pltpu.VMEM((nreq, 8, slots), jnp.float32),
            dma((chunks,)),
            dma((nvoc,)),
            dma((nz,)),
            dma((nz,)),
            dma((nz,)),
            dma((nvoc,)),
            dma((nvoc,)),
            dma((nvoc,)),
            dma((nvoc,)),
            dma((nvoc,)),
            dma((nvoc,)),
            dma((nreq,)),
            dma((nreq,)),
        ],
        compiler_params=pltpu.CompilerParams(
            collective_id=0, has_side_effects=True, vmem_limit_bytes=48 * 1024 * 1024
        ),
        cost_estimate=pl.CostEstimate(
            flops=2 * nvoc * LIVE * depth * width,
            bytes_accessed=2 * depth * width,
            transcendentals=nvoc * LIVE * width,
        ),
    )(bounds, hidden, norm_gain.reshape(1, depth), targets.reshape(1, slots), head)
    return tuple(a.reshape(-1) for a in outs)


def solution(mesh):
    placed = (
        P(("req", "voc"), None),
        P(),
        P(None, "voc"),
        P(("req", "voc")),
        P(("req", "voc"), None),
    )
    return jax.shard_map(
        functools.partial(shards, mesh.shape["req"], mesh.shape["voc"]),
        mesh=mesh,
        in_specs=placed,
        out_specs=(P(("req", "voc")), P(("req", "voc")), P(("req", "voc")), P()),
        check_vma=False,
    )
```

time: 283 us -> 57.7 us (0.20)
  blocking collectives: 181 us -> 0 us
  Pallas kernels: 0 us -> 50.6 us
  waiting for transfers between devices: 37.6 us -> 0 us
  matrix products: 27.5 us -> 0 us
  other arithmetic: 15.8 us -> 0 us
  between operations: 16.7 us -> 2.38 us
    all_gather x5 -> x0, blocking collectives: 144 us -> none  [the longest x4 122 us: joined(): gathered = jax.tree.map(lambda a: lax.all_gather(a, axis), part)]
    pallas_call x0 -> x1, Pallas kernels: none -> 50.6 us  [shards(): pl.pallas_call(functools.partial(kernel, nreq, nvoc), out_shape=(line, li...]
    all_gather x1 -> x0, waiting for transfers between devices: 37.6 us -> none  [shards(): lax.all_gather(normed, 'voc', axis=0, tiled=True)]
    psum x1 -> x0, blocking collectives: 37.5 us -> none  [shards(): lax.psum((jnp.sum(entropy), jnp.sum(live.astype(jnp.float32))), ('req', '...]
    dot_general x2 -> x0, matrix products: 27.5 us -> none  [one_block(): logits = jnp.dot(rows_in, head, preferred_element_type=jnp.float32)]
    reduce_sum x5 -> x0, other arithmetic: 13.6 us -> none  [the longest x2 9.39 us: one_block(): weighted = jnp.sum(expo * logits, axis=-1)]
    unnamed x8 -> x9, local copies, waits for them, and re-layouts: 0.1 us -> 3.84 us
  transfers between devices with their start and end apart: 1 -> 0, of which waited for: 1 -> 0; matrix products, arithmetic and copies ran while one was open for 1% -> 0% of each run, Pallas kernels for 0% -> 0%
where the time goes in v1:
time: 57.7 us; the launch traced here: 57.5 us
  Pallas kernels  50.6 us (88%)
  local copies, waits for them, and re-layouts  4.54 us (8%)
  between operations  2.38 us (4%)
    pallas_call x1, Pallas kernels, shards(): pl.pallas_call(functools.partial(kernel, nreq, nvoc), out_shape=(line, li...  50.6 us
    unnamed x9, local copies, waits for them, and re-layouts  3.84 us

profile of v1, /device:TPU:0, one launch (start us, length us, event | category | flops | bytes accessed | tf_op | source)
XLA Modules:
  0.0 57.5 jit_solution(14902959201833497875)
XLA Ops:
  0.6 0.7 %reshape.26.gain = f32[1,1536]{1,0:T(1,128)S(1)} reshape(f32[1536]{0:T(1024)} %param.6) | data formatting | bytes 12288 | tf_op jit(solution)/shard_map/reshape | solution.py:378
  1.3 0.0 copy-start
  1.3 1.0 %copy-done = bf16[128,1536]{1,0:T(8,128)(2,1)S(1)} copy-done((bf16[128,1536]{1,0:T(8,128)(2,1)S(1)}, bf16[128,1536]{1,0:T(8,128)(2,1)}, u32[]{:S(2)}) %copy-start) | copy-done | bytes 393240
  2.3 0.0 copy-start.1
  2.3 0.7 %copy-done.1 = s32[1,2]{1,0:T(1,128)S(1)} copy-done((s32[1,2]{1,0:T(1,128)S(1)}, s32[1,2]{1,0:T(1,128)}, u32[]{:S(2)}) %copy-start.1) | copy-done | bytes 32
  3.0 0.0 copy-start.2
  3.0 0.7 %copy-done.2 = s32[128]{0:T(128)S(1)} copy-done((s32[128]{0:T(128)S(1)}, s32[128]{0:T(128)}, u32[]{:S(2)}) %copy-start.2) | copy-done | bytes 536
  3.6 50.6 %shard_map.84 = (f32[1,128]{1,0:T(1,128)S(1)}, f32[1,128]{1,0:T(1,128)S(1)}, f32[1,128]{1,0:T(1,128)S(1)}, f32[1,1]{1,0:T(1,128)}) custom-call(s32[1,2]{1,0:T(1,128)S(1)} %copy-done.1, bf16[128,1536]{1,0:T(8,128)(2,1)S(1)} %copy-done, f32[1,1536]{1,0:T(1,128)S(1)} %reshape.26.gain, s32[1,128]{1,0:T(1,128)S(1)} %bitcast.5, bf16[1536,6144]{1,0:T(8,128)(2,1)} %head.1), custom_call_target="tpu_custom_call" | custom-call | flops 14495514624 | bytes 18874368 | tf_op jit(solution)/shard_map/pallas_call | solution.py:334
  54.2 0.5 copy.13
  54.7 0.5 copy.14
  55.2 0.5 copy.15
Async XLA Ops:
  1.3 1.0 %copy-start = (bf16[128,1536]{1,0:T(8,128)(2,1)S(1)}, bf16[128,1536]{1,0:T(8,128)(2,1)}, u32[]{:S(2)}) copy-start(bf16[128,1536]{1,0:T(8,128)(2,1)} %hidden.1) | copy-start | bytes 1179652
  2.3 0.7 %copy-start.1 = (s32[1,2]{1,0:T(1,128)S(1)}, s32[1,2]{1,0:T(1,128)}, u32[]{:S(2)}) copy-start(s32[1,2]{1,0:T(1,128)} %bounds.1) | copy-start | bytes 28
  3.0 0.7 %copy-start.2 = (s32[128]{0:T(128)S(1)}, s32[128]{0:T(128)}, u32[]{:S(2)}) copy-start(s32[128]{0:T(128)} %param.8) | copy-start | bytes 1540

commit v2 on v1

--- a/solution.py
+++ b/solution.py
@@ -8,6 +8,7 @@
 from jax.sharding import PartitionSpec as P
 
 LIVE = 96
+HALF = LIVE // 2
 SIDE = 2
 LANES = 128
 CHUNK = 768
@@ -15,10 +16,10 @@
 
 
 def kernel(
-    nreq, nvoc, bounds, hidden, gain, targets, head, logprob, entropy, picked_out, mean,
-    rows, weights, first, second, top, total, weighted, picked, group,
+    nreq, nvoc, hidden_in, gain_in, targets_in, bounds_in, head, out,
+    hidden, gain, targets, bounds, rows, weights, first, second, top, total, weighted, picked, group,
     meta, stats, stats_out, ent, ent_sum,
-    head_sem, rows_rx, down_tx, up_tx, side_tx, meta_rx, meta_tx, stats_rx, stats_tx,
+    in_sem, head_sem, rows_rx, down_tx, up_tx, side_tx, extra_tx, meta_rx, meta_tx, stats_rx, stats_tx,
     ent_rx, ent_tx, sum_rx, sum_tx,
 ):
     nz = nvoc // SIDE
@@ -40,6 +41,14 @@
             head.at[:, pl.ds(pl.multiple_of(c * CHUNK, CHUNK), CHUNK)], weights.at[c], head_sem.at[c]
         )
 
+    loads = [
+        pltpu.make_async_copy(source, target, in_sem.at[n])
+        for n, (source, target) in enumerate(
+            ((hidden_in, hidden), (gain_in, gain), (targets_in, targets), (bounds_in, bounds))
+        )
+    ]
+    for load in loads:
+        load.start()
     barrier = pltpu.get_barrier_semaphore()
     for i in range(1, nvoc):
         pl.semaphore_signal(barrier, inc=1, device_id={"voc": lax.rem(me + i, nvoc)})
@@ -49,34 +58,50 @@
     for c in range(chunks):
         load_head(c).start()
 
-    lo = bounds[0, 0]
-    hi = bounds[0, 1]
+    for load in loads:
+        load.wait()
+    lo = bounds[0:1, 0:1]
+    hi = bounds[0:1, 1:2]
     values = hidden[...].astype(jnp.float32)
     meansq = jnp.mean(values * values, axis=-1, keepdims=True)
-    normed = (values * lax.rsqrt(meansq + 1e-05) * gain[...]).astype(jnp.bfloat16)
+    values = values * lax.rsqrt(meansq + 1e-05)
+    normed = jnp.concatenate(
+        [values[:, j * LANES : (j + 1) * LANES] * gain[j : j + 1, :] for j in range(gain.shape[0])],
+        axis=1,
+    ).astype(jnp.bfloat16)
     slot = lax.broadcasted_iota(jnp.int32, (LIVE, slots), 1)
     order = lax.broadcasted_iota(jnp.int32, (LIVE, slots), 0)
     window = jnp.where(slot == order + lo, 1.0, 0.0).astype(jnp.bfloat16)
     rows[me] = jnp.dot(window, normed, preferred_element_type=jnp.float32).astype(jnp.bfloat16)
     tile_row = lax.broadcasted_iota(jnp.int32, (8, slots), 0)
-    meta[me] = jnp.where(tile_row == 0, jnp.broadcast_to(targets[...], (8, slots)), lo)
+    meta[me] = jnp.where(tile_row == 0, jnp.broadcast_to(targets[...], (8, slots)), jnp.broadcast_to(lo, (8, slots)))
 
     pl.semaphore_wait(barrier, nvoc - 1 + nreq - 1)
 
-    def send_rows(source, target, sem):
+    def send_rows(block, half, target, sem):
+        piece = rows.at[block, pl.ds(half * HALF, HALF)]
         return pltpu.make_async_remote_copy(
-            src_ref=rows.at[source], dst_ref=rows.at[source], send_sem=sem,
-            recv_sem=rows_rx.at[source], device_id={"voc": target},
-        )
-
-    def send_down(place):
-        return send_rows(at(place, x), at(z - 1, x), down_tx.at[place])
-
-    def send_up(place):
-        return send_rows(at(place, x), at(z + 1, x), up_tx.at[place])
-
-    def send_side(place):
-        return send_rows(at(place, x), partner, side_tx.at[place])
+            src_ref=piece, dst_ref=piece, send_sem=sem,
+            recv_sem=rows_rx.at[block, half], device_id={"voc": target},
+        )
+
+    def send_down(place, half):
+        return send_rows(at(place, x), half, at(z - 1, x), down_tx.at[place, half])
+
+    def send_up(place, half):
+        return send_rows(at(place, x), half, at(z + 1, x), up_tx.at[place, half])
+
+    def send_side(place, half):
+        return send_rows(at(place, x), half, partner, side_tx.at[place, half])
+
+    def extra_up():
+        return send_rows(at(0, SIDE - 1 - x), 1, at(z + 1, x), extra_tx.at[0])
+
+    def extra_down():
+        return send_rows(at(nz - 1, SIDE - 1 - x), 1, at(z - 1, x), extra_tx.at[1])
+
+    def wait_rows(block, half):
+        send_rows(block, half, partner, side_tx.at[0, 0]).wait_recv()
 
     def send_meta(i):
         return pltpu.make_async_remote_copy(
@@ -84,15 +109,16 @@
             recv_sem=meta_rx.at[me], device_id={"voc": lax.rem(me + i, nvoc)},
         )
 
-    @pl.when(z > 0)
-    def _():
-        send_down(z).start()
-
-    @pl.when(z < nz - 1)
-    def _():
-        send_up(z).start()
-
-    send_side(z).start()
+    for half in range(2):
+        @pl.when(z > 0)
+        def _():
+            send_down(z, half).start()
+
+        @pl.when(z < nz - 1)
+        def _():
+            send_up(z, half).start()
+
+        send_side(z, half).start()
     for i in range(1, nvoc):
         send_meta(i).start()
 
@@ -153,7 +179,57 @@
         lines = [jnp.sum(jnp.where(hit, col, 0.0), axis=0, keepdims=True) for col in columns]
         return jnp.concatenate(lines + [jnp.zeros((4, slots), jnp.float32)], axis=0)
 
-    def work(blocks, fresh):
+    def forward(t, half):
+        @pl.when(z - t >= 0)
+        def _():
+            wait_rows(at(z - t, x), half)
+
+            @pl.when(z < nz - 1)
+            def _():
+                send_up(z - t, half).start()
+
+            @pl.when((half == 0) | (z - t > 0))
+            def _():
+                send_side(z - t, half).start()
+
+        @pl.when(z + t < nz)
+        def _():
+            wait_rows(at(z + t, x), half)
+
+            @pl.when(z > 0)
+            def _():
+                send_down(z + t, half).start()
+
+            @pl.when((half == 0) | (z + t < nz - 1))
+            def _():
+                send_side(z + t, half).start()
+
+        gap = t - 1
+        due = (t == 1) if half == 1 else (t > 1)
+
+        @pl.when(due & (z == gap))
+        def _():
+            wait_rows(at(0, SIDE - 1 - x), 1)
+            extra_up().start()
+
+        @pl.when(due & (nz - 1 - z == gap))
+        def _():
+            wait_rows(at(nz - 1, SIDE - 1 - x), 1)
+            extra_down().start()
+
+    def wait_across(place):
+        block = at(place, SIDE - 1 - x)
+        wait_rows(block, 0)
+        inner = (place > 0) & (place < nz - 1)
+        opposite = (place - z == nz - 1) | (z - place == nz - 1)
+
+        @pl.when(inner | opposite)
+        def _():
+            wait_rows(block, 1)
+
+    def work(blocks, fresh, middle=None):
+        steps = chunks // 2 - 1
+
         def ready(c):
             if fresh:
                 load_head(c).wait()
@@ -163,6 +239,8 @@
         multiply(blocks, 0, first)
 
         def body(i, carry):
+            if middle is not None:
+                pl.when(i == min(2, steps - 1))(middle)
             c = i * 2
             ready(c + 1)
             multiply(blocks, c + 1, second)
@@ -172,7 +250,7 @@
             absorb(len(blocks), c + 1, second)
             return carry
 
-        lax.fori_loop(0, chunks // 2 - 1, body, 0)
+        lax.fori_loop(0, steps, body, 0)
         ready(chunks - 1)
         multiply(blocks, chunks - 1, second)
         absorb(len(blocks), chunks - 2, first)
@@ -194,9 +272,6 @@
             recv_sem=meta_rx.at[block], device_id={"voc": partner},
         ).wait_recv()
 
-    def wait_rows(block):
-        send_rows(block, partner, side_tx.at[0]).wait_recv()
-
     near = jnp.minimum(z, nz - 1 - z)
     far_side = jnp.where(z > nz - 1 - z, -1, 1)
 
@@ -206,43 +281,36 @@
         side = jnp.where(close, 2 * lax.rem(i, 2) - 1, far_side)
         return z + side * step
 
-    work([me], True)
+    work([me], True, lambda: forward(1, 0))
     stats[me] = block_stats(0, me)
+    forward(1, 1)
 
     def tick(t, carry):
-        @pl.when(z - t >= 0)
-        def _():
-            wait_rows(at(z - t, x))
-
-            @pl.when(z < nz - 1)
-            def _():
-                send_up(z - t).start()
-
-            send_side(z - t).start()
-
-        @pl.when(z + t < nz)
-        def _():
-            wait_rows(at(z + t, x))
-
-            @pl.when(z > 0)
-            def _():
-                send_down(z + t).start()
-
-            send_side(z + t).start()
-
-        across = at(jnp.where(t == 1, z, line(jnp.maximum(t - 2, 0))), SIDE - 1 - x)
+        place = jnp.where(t == 1, z, line(jnp.maximum(t - 2, 0)))
+        across = at(place, SIDE - 1 - x)
         along = at(line(t - 1), x)
-        wait_rows(across)
+        wait_across(place)
         wait_meta(across)
         wait_meta(along)
-        work([across, along], False)
+
+        def middle():
+            @pl.when(t + 1 < nz)
+            def _():
+                forward(t + 1, 0)
+
+        work([across, along], False, middle)
+
+        @pl.when(t + 1 < nz)
+        def _():
+            forward(t + 1, 1)
+
         give(0, across)
         give(1, along)
         return carry
 
     lax.fori_loop(1, nz, tick, 0)
     last = at(line(nz - 2), SIDE - 1 - x)
-    wait_rows(last)
+    wait_across(line(nz - 2))
     wait_meta(last)
     work([last], False)
     give(0, last)
@@ -263,9 +331,8 @@
     live = (place >= lo) & (place < hi)
     lse = best + jnp.log(all_total)
     row_entropy = jnp.where(live, lse - all_weighted / all_total, 0.0)
-    logprob[...] = jnp.where(live, chosen - lse, 0.0)
-    entropy[...] = row_entropy
-    picked_out[...] = jnp.where(live, chosen, 0.0)
+    row_logprob = jnp.where(live, chosen - lse, 0.0)
+    row_picked = jnp.where(live, chosen, 0.0)
 
     ent[me] = jnp.concatenate(
         [row_entropy, jnp.where(live, 1.0, 0.0), jnp.zeros((6, slots), jnp.float32)], axis=0
@@ -301,18 +368,19 @@
             recv_sem=sum_rx.at[source], device_id={"req": source},
         ).wait_recv()
     summed = jnp.sum(functools.reduce(jnp.add, [ent_sum[i] for i in range(nreq)]), axis=-1, keepdims=True)
-    mean[...] = summed[0:1] / summed[1:2]
+    mean = jnp.broadcast_to(summed[0:1] / summed[1:2], (1, slots))
+    out[...] = jnp.concatenate([row_logprob, row_entropy, row_picked, mean], axis=0)
 
     for place in range(nz):
-        send_side(place).wait_send()
-
-        @pl.when((z > 0) & (z <= place))
-        def _():
-            send_down(place).wait_send()
-
-        @pl.when((z < nz - 1) & (z >= place))
-        def _():
-            send_up(place).wait_send()
+        for half in range(2):
+            if half == 0 or 0 < place < nz - 1:
+                send_side(place, half).wait_send()
+            else:
+                pl.when(z == place)(lambda: send_side(place, half).wait_send())
+            pl.when((z > 0) & (z <= place))(lambda: send_down(place, half).wait_send())
+            pl.when((z < nz - 1) & (z >= place))(lambda: send_up(place, half).wait_send())
+    pl.when(z < nz - 1)(lambda: extra_up().wait_send())
+    pl.when(z > 0)(lambda: extra_down().wait_send())
 
     for i in range(1, nvoc):
         send_meta(i).wait_send()
@@ -329,16 +397,18 @@
     chunks = width // CHUNK
     pair = 2 * LIVE
     vmem = pl.BlockSpec(memory_space=pltpu.VMEM)
-    line = jax.ShapeDtypeStruct((1, slots), jnp.float32)
+    anywhere = pl.BlockSpec(memory_space=pl.ANY)
     dma = pltpu.SemaphoreType.DMA
-    outs = pl.pallas_call(
+    out = pl.pallas_call(
         functools.partial(kernel, nreq, nvoc),
-        out_shape=(line, line, line, jax.ShapeDtypeStruct((1, 1), jnp.float32)),
-        in_specs=[
-            pl.BlockSpec(memory_space=pltpu.SMEM), vmem, vmem, vmem, pl.BlockSpec(memory_space=pl.ANY),
-        ],
-        out_specs=(vmem, vmem, vmem, vmem),
+        out_shape=jax.ShapeDtypeStruct((4, slots), jnp.float32),
+        in_specs=[anywhere] * 5,
+        out_specs=vmem,
         scratch_shapes=[
+            pltpu.VMEM((slots, depth), jnp.bfloat16),
+            pltpu.VMEM((depth // LANES, LANES), jnp.float32),
+            pltpu.VMEM((1, slots), jnp.int32),
+            pltpu.VMEM((1, 2), jnp.int32),
             pltpu.VMEM((nvoc, LIVE, depth), jnp.bfloat16),
             pltpu.VMEM((chunks, depth, CHUNK), jnp.bfloat16),
             pltpu.VMEM((pair, CHUNK), jnp.float32),
@@ -353,11 +423,13 @@
             pltpu.VMEM((nvoc, 8, slots), jnp.float32),
             pltpu.VMEM((nvoc, 8, slots), jnp.float32),
             pltpu.VMEM((nreq, 8, slots), jnp.float32),
+            dma((4,)),
             dma((chunks,)),
-            dma((nvoc,)),
-            dma((nz,)),
-            dma((nz,)),
-            dma((nz,)),
+            dma((nvoc, 2)),
+            dma((nz, 2)),
+            dma((nz, 2)),
+            dma((nz, 2)),
+            dma((2,)),
             dma((nvoc,)),
             dma((nvoc,)),
             dma((nvoc,)),
@@ -368,15 +440,15 @@
             dma((nreq,)),
         ],
         compiler_params=pltpu.CompilerParams(
-            collective_id=0, has_side_effects=True, vmem_limit_bytes=48 * 1024 * 1024
+            collective_id=0, has_side_effects=True, vmem_limit_bytes=60 * 1024 * 1024
         ),
         cost_estimate=pl.CostEstimate(
             flops=2 * nvoc * LIVE * depth * width,
             bytes_accessed=2 * depth * width,
             transcendentals=nvoc * LIVE * width,
         ),
-    )(bounds, hidden, norm_gain.reshape(1, depth), targets.reshape(1, slots), head)
-    return tuple(a.reshape(-1) for a in outs)
+    )(hidden, norm_gain.reshape(depth // LANES, LANES), targets.reshape(1, slots), bounds, head)
+    return out[0], out[1], out[2], out[3, :1]
 
 
 def solution(mesh):

time: 57.7 us -> 53.9 us (0.934)
  local copies, waits for them, and re-layouts: 4.54 us -> 2.49 us
  between operations: 2.38 us -> 0.64 us
    unnamed x9 -> x0, local copies, waits for them, and re-layouts: 3.84 us -> none
    squeeze x0 -> x1, local copies, waits for them, and re-layouts: none -> 1.3 us  [shards(): return (out[0], out[1], out[2], out[3, :1])]
    slice x0 -> x1, local copies, waits for them, and re-layouts: none -> 1.18 us  [shards(): return (out[0], out[1], out[2], out[3, :1])]
    reshape x1 -> x0, local copies, waits for them, and re-layouts: 0.7 us -> none  [shards(): norm_gain.reshape(1, depth)]
where the time goes in v2:
time: 53.9 us; the launch traced here: 53.8 us
  Pallas kernels  50.6 us (94%)
  local copies, waits for them, and re-layouts  2.49 us (5%)
  between operations  0.64 us (1%)
    pallas_call x1, Pallas kernels, shards(): pl.pallas_call(functools.partial(kernel, nreq, nvoc), out_shape=jax.Shape...  50.6 us
    squeeze x1, local copies, waits for them, and re-layouts, shards(): return (out[0], out[1], out[2], out[3, :1])  1.3 us
    slice x1, local copies, waits for them, and re-layouts, shards(): return (out[0], out[1], out[2], out[3, :1])  1.18 us

profile of v2, /device:TPU:0, one launch (start us, length us, event | category | flops | bytes accessed | tf_op | source)
XLA Modules:
  0.0 53.8 jit_solution(16388953261700928172)
XLA Ops:
  0.6 50.6 %shard_map.84 = f32[4,128]{1,0:T(4,128)} custom-call(bf16[128,1536]{1,0:T(8,128)(2,1)} %hidden_in.1, f32[12,128]{1,0:T(8,128)} %bitcast.9, s32[1,128]{1,0:T(1,128)} %bitcast.10, s32[1,2]{1,0:T(1,128)} %bounds_in.1, bf16[1536,6144]{1,0:T(8,128)(2,1)} %head.1), custom_call_target="tpu_custom_call" | custom-call | flops 14495514624 | bytes 18874368 | tf_op jit(solution)/shard_map/pallas_call | solution.py:402
  51.3 1.3 %slice_bitcast_fusion = (f32[128]{0:T(128)}, f32[128]{0:T(128)}, f32[128]{0:T(128)}) fusion(f32[4,128]{1,0:T(4,128)} %shard_map.84), kind=kLoop, calls=%fused_computation | loop fusion | bytes 3072 | tf_op jit(solution)/shard_map/squeeze | solution.py:451
  52.6 1.2 %slice.15 = f32[1,1]{1,0:T(1,128)} slice(f32[4,128]{1,0:T(4,128)} %shard_map.84), slice={[3:4], [0:1]} | slice | bytes 8 | tf_op jit(solution)/shard_map/slice | solution.py:451

commit v3 on v2

--- a/solution.py
+++ b/solution.py
@@ -12,6 +12,9 @@
 SIDE = 2
 LANES = 128
 CHUNK = 768
+PART = 256
+PARTS = CHUNK // PART
+TICKS = 2
 LOW = -1e30
 
 
@@ -138,15 +141,17 @@
         for state in (total, weighted, picked):
             state[pl.ds(0, size), :] = jnp.zeros((size, LANES), jnp.float32)
 
-    def multiply(blocks, c, out):
+    def multiply(blocks, c, out, n):
         left = [rows[block] for block in blocks]
         left = left[0] if len(left) == 1 else jnp.concatenate(left, axis=0)
-        out[pl.ds(0, len(blocks) * LIVE), :] = jnp.dot(
-            left, weights[c], preferred_element_type=jnp.float32
-        )
-
-    def absorb(count, c, logits):
-        for r in range(0, count * LIVE, 8):
+        here = pl.ds(n * PART, PART)
+        out[pl.ds(0, len(blocks) * LIVE), here] = jnp.dot(
+            left, weights[c, :, here], preferred_element_type=jnp.float32
+        )
+
+    def absorb(count, c, logits, n):
+        share = count * LIVE // PARTS
+        for r in range(n * share, (n + 1) * share, 8):
             here = pl.ds(r, 8)
             part = [logits[here, pl.ds(j * LANES, LANES)] for j in range(cells)]
             old = top[here, :]
@@ -205,14 +210,15 @@
                 send_side(z + t, half).start()
 
         gap = t - 1
-        due = (t == 1) if half == 1 else (t > 1)
-
-        @pl.when(due & (z == gap))
+        if (t == 1) != (half == 1):
+            return
+
+        @pl.when(z == gap)
         def _():
             wait_rows(at(0, SIDE - 1 - x), 1)
             extra_up().start()
 
-        @pl.when(due & (nz - 1 - z == gap))
+        @pl.when(nz - 1 - z == gap)
         def _():
             wait_rows(at(nz - 1, SIDE - 1 - x), 1)
             extra_down().start()
@@ -227,34 +233,43 @@
         def _():
             wait_rows(block, 1)
 
-    def work(blocks, fresh, middle=None):
+    def work(blocks, fresh, events=()):
         steps = chunks // 2 - 1
+        count = len(blocks)
 
         def ready(c):
             if fresh:
                 load_head(c).wait()
 
+        def both(c, ahead, behind):
+            for n in range(PARTS):
+                multiply(blocks, c, ahead, n)
+                absorb(count, c - 1, behind, n)
+
         prepare(blocks)
         ready(0)
-        multiply(blocks, 0, first)
+        for n in range(PARTS):
+            multiply(blocks, 0, first, n)
 
         def body(i, carry):
-            if middle is not None:
-                pl.when(i == min(2, steps - 1))(middle)
+            for when, event in events:
+                if when < steps:
+                    pl.when(i == when)(event)
             c = i * 2
             ready(c + 1)
-            multiply(blocks, c + 1, second)
-            absorb(len(blocks), c, first)
+            both(c + 1, second, first)
             ready(c + 2)
-            multiply(blocks, c + 2, first)
-            absorb(len(blocks), c + 1, second)
+            both(c + 2, first, second)
             return carry
 
         lax.fori_loop(0, steps, body, 0)
         ready(chunks - 1)
-        multiply(blocks, chunks - 1, second)
-        absorb(len(blocks), chunks - 2, first)
-        absorb(len(blocks), chunks - 1, second)
+        both(chunks - 1, second, first)
+        for n in range(PARTS):
+            absorb(count, chunks - 1, second, n)
+        for when, event in events:
+            if when >= steps:
+                event()
 
     def send_stats(block):
         return pltpu.make_async_remote_copy(
@@ -278,42 +293,33 @@
     def line(i):
         close = i < 2 * near
         step = jnp.where(close, i // 2 + 1, i - near + 1)
-        side = jnp.where(close, 2 * lax.rem(i, 2) - 1, far_side)
+        side = jnp.where(close, 2 * (i % 2) - 1, far_side)
         return z + side * step
 
-    work([me], True, lambda: forward(1, 0))
+    def forwards(t):
+        return [functools.partial(forward, t, half) for half in range(2)] if t < nz else []
+
+    work([me], True, list(zip((2, chunks), forwards(1))))
     stats[me] = block_stats(0, me)
-    forward(1, 1)
-
-    def tick(t, carry):
-        place = jnp.where(t == 1, z, line(jnp.maximum(t - 2, 0)))
-        across = at(place, SIDE - 1 - x)
-        along = at(line(t - 1), x)
-        wait_across(place)
-        wait_meta(across)
-        wait_meta(along)
-
-        def middle():
-            @pl.when(t + 1 < nz)
-            def _():
-                forward(t + 1, 0)
-
-        work([across, along], False, middle)
-
-        @pl.when(t + 1 < nz)
-        def _():
-            forward(t + 1, 1)
-
-        give(0, across)
-        give(1, along)
-        return carry
-
-    lax.fori_loop(1, nz, tick, 0)
-    last = at(line(nz - 2), SIDE - 1 - x)
-    wait_across(line(nz - 2))
-    wait_meta(last)
-    work([last], False)
-    give(0, last)
+
+    for begin in range(1, nz, TICKS):
+        end = min(begin + TICKS, nz)
+        for t in range(begin + 1, end):
+            for event in forwards(t):
+                event()
+        blocks = []
+        for t in range(begin, end):
+            place = z if t == 1 else line(t - 2)
+            wait_across(place)
+            blocks += [at(place, SIDE - 1 - x), at(line(t - 1), x)]
+        if end == nz:
+            wait_across(line(nz - 2))
+            blocks.append(at(line(nz - 2), SIDE - 1 - x))
+        for block in blocks:
+            wait_meta(block)
+        work(blocks, False, list(zip((1, 2), forwards(end))))
+        for n, block in enumerate(blocks):
+            give(n, block)
 
     for i in range(1, nvoc):
         source = lax.rem(me + i, nvoc)
@@ -395,7 +401,7 @@
     width = head.shape[1]
     nz = nvoc // SIDE
     chunks = width // CHUNK
-    pair = 2 * LIVE
+    pair = (2 * TICKS + 1) * LIVE
     vmem = pl.BlockSpec(memory_space=pltpu.VMEM)
     anywhere = pl.BlockSpec(memory_space=pl.ANY)
     dma = pltpu.SemaphoreType.DMA

time: 53.9 us -> 56.6 us (1.050)
  Pallas kernels: 50.6 us -> 53.3 us
    pallas_call x1, Pallas kernels: 50.6 us -> 53.3 us  [shards(): pl.pallas_call(functools.partial(kernel, nreq, nvoc), out_shape=jax.Shape...]
where the time goes in v3:
time: 56.6 us; the launch traced here: 56.4 us
  Pallas kernels  53.3 us (94%)
  local copies, waits for them, and re-layouts  2.49 us (4%)
  between operations  0.64 us (1%)
    pallas_call x1, Pallas kernels, shards(): pl.pallas_call(functools.partial(kernel, nreq, nvoc), out_shape=jax.Shape...  53.3 us
    squeeze x1, local copies, waits for them, and re-layouts, shards(): return (out[0], out[1], out[2], out[3, :1])  1.3 us
    slice x1, local copies, waits for them, and re-layouts, shards(): return (out[0], out[1], out[2], out[3, :1])  1.18 us

profile of v3, /device:TPU:0, one launch (start us, length us, event | category | flops | bytes accessed | tf_op | source)
XLA Modules:
  0.0 56.4 jit_solution(15125139479219128370)
XLA Ops:
  0.6 53.3 %shard_map.84 = f32[4,128]{1,0:T(4,128)} custom-call(bf16[128,1536]{1,0:T(8,128)(2,1)} %hidden_in.1, f32[12,128]{1,0:T(8,128)} %bitcast.9, s32[1,128]{1,0:T(1,128)} %bitcast.10, s32[1,2]{1,0:T(1,128)} %bounds_in.1, bf16[1536,6144]{1,0:T(8,128)(2,1)} %head.1), custom_call_target="tpu_custom_call" | custom-call | flops 14495514624 | bytes 18874368 | tf_op jit(solution)/shard_map/pallas_call | solution.py:408
  53.9 1.3 %slice_bitcast_fusion = (f32[128]{0:T(128)}, f32[128]{0:T(128)}, f32[128]{0:T(128)}) fusion(f32[4,128]{1,0:T(4,128)} %shard_map.84), kind=kLoop, calls=%fused_computation | loop fusion | bytes 3072 | tf_op jit(solution)/shard_map/squeeze | solution.py:457
  55.2 1.2 %slice.15 = f32[1,1]{1,0:T(1,128)} slice(f32[4,128]{1,0:T(4,128)} %shard_map.84), slice={[3:4], [0:1]} | slice | bytes 8 | tf_op jit(solution)/shard_map/slice | solution.py:457

commit v4 on v2

--- a/solution.py
+++ b/solution.py
@@ -12,7 +12,17 @@
 SIDE = 2
 LANES = 128
 CHUNK = 768
+PART = 256
+PARTS = CHUNK // PART
+STEP = 32
 LOW = -1e30
+
+
+def tree(combine, values):
+    while len(values) > 1:
+        pairs = [combine(a, b) for a, b in zip(values[::2], values[1::2])]
+        values = pairs + values[len(pairs) * 2 :]
+    return values[0]
 
 
 def kernel(
@@ -138,30 +148,34 @@
         for state in (total, weighted, picked):
             state[pl.ds(0, size), :] = jnp.zeros((size, LANES), jnp.float32)
 
-    def multiply(blocks, c, out):
+    def multiply(blocks, c, out, n):
         left = [rows[block] for block in blocks]
         left = left[0] if len(left) == 1 else jnp.concatenate(left, axis=0)
-        out[pl.ds(0, len(blocks) * LIVE), :] = jnp.dot(
-            left, weights[c], preferred_element_type=jnp.float32
-        )
-
-    def absorb(count, c, logits):
-        for r in range(0, count * LIVE, 8):
-            here = pl.ds(r, 8)
+        here = pl.ds(n * PART, PART)
+        out[pl.ds(0, len(blocks) * LIVE), here] = jnp.dot(
+            left, weights[c, :, here], preferred_element_type=jnp.float32
+        )
+
+    def absorb(count, c, logits, n):
+        share = count * LIVE // PARTS
+        for r in range(n * share, (n + 1) * share, STEP):
+            here = pl.ds(r, STEP)
             part = [logits[here, pl.ds(j * LANES, LANES)] for j in range(cells)]
             old = top[here, :]
-            new = functools.reduce(jnp.maximum, part, old)
+            old_total = total[here, :]
+            old_weighted = weighted[here, :]
+            found = picked[here, :]
+            wanted = group[here, :]
+            new = tree(jnp.maximum, part + [old])
             scale = jnp.exp(old - new)
             expo = [jnp.exp(v - new) for v in part]
-            top[here, :] = new
-            total[here, :] = total[here, :] * scale + functools.reduce(jnp.add, expo)
-            weighted[here, :] = weighted[here, :] * scale + functools.reduce(
-                jnp.add, [e * v for e, v in zip(expo, part)]
-            )
-            wanted = group[here, :]
-            found = picked[here, :]
             for j, v in enumerate(part):
                 found = jnp.where(wanted == c * cells + j, v, found)
+            new_total = old_total * scale + tree(jnp.add, expo)
+            new_weighted = old_weighted * scale + tree(jnp.add, [e * v for e, v in zip(expo, part)])
+            top[here, :] = new
+            total[here, :] = new_total
+            weighted[here, :] = new_weighted
             picked[here, :] = found
 
     def block_stats(n, block):
@@ -234,27 +248,33 @@
             if fresh:
                 load_head(c).wait()
 
+        count = len(blocks)
+
+        def both(c, ahead, behind):
+            for n in range(PARTS):
+                multiply(blocks, c, ahead, n)
+                absorb(count, c - 1, behind, n)
+
         prepare(blocks)
         ready(0)
-        multiply(blocks, 0, first)
+        for n in range(PARTS):
+            multiply(blocks, 0, first, n)
 
         def body(i, carry):
             if middle is not None:
                 pl.when(i == min(2, steps - 1))(middle)
             c = i * 2
             ready(c + 1)
-            multiply(blocks, c + 1, second)
-            absorb(len(blocks), c, first)
+            both(c + 1, second, first)
             ready(c + 2)
-            multiply(blocks, c + 2, first)
-            absorb(len(blocks), c + 1, second)
+            both(c + 2, first, second)
             return carry
 
         lax.fori_loop(0, steps, body, 0)
         ready(chunks - 1)
-        multiply(blocks, chunks - 1, second)
-        absorb(len(blocks), chunks - 2, first)
-        absorb(len(blocks), chunks - 1, second)
+        both(chunks - 1, second, first)
+        for n in range(PARTS):
+            absorb(count, chunks - 1, second, n)
 
     def send_stats(block):
         return pltpu.make_async_remote_copy(

time: 53.9 us -> 53.8 us (level)
  no operation moved by 1% of the time
where the time goes in v4:
time: 53.8 us; the launch traced here: 53.6 us
  Pallas kernels  50.4 us (94%)
  local copies, waits for them, and re-layouts  2.49 us (5%)
  between operations  0.64 us (1%)
    pallas_call x1, Pallas kernels, shards(): pl.pallas_call(functools.partial(kernel, nreq, nvoc), out_shape=jax.Shape...  50.4 us
    squeeze x1, local copies, waits for them, and re-layouts, shards(): return (out[0], out[1], out[2], out[3, :1])  1.3 us
    slice x1, local copies, waits for them, and re-layouts, shards(): return (out[0], out[1], out[2], out[3, :1])  1.18 us

profile of v4, /device:TPU:0, one launch (start us, length us, event | category | flops | bytes accessed | tf_op | source)
XLA Modules:
  0.0 53.6 jit_solution(13942311678890286269)
XLA Ops:
  0.6 50.4 %shard_map.84 = f32[4,128]{1,0:T(4,128)} custom-call(bf16[128,1536]{1,0:T(8,128)(2,1)} %hidden_in.1, f32[12,128]{1,0:T(8,128)} %bitcast.9, s32[1,128]{1,0:T(1,128)} %bitcast.10, s32[1,2]{1,0:T(1,128)} %bounds_in.1, bf16[1536,6144]{1,0:T(8,128)(2,1)} %head.1), custom_call_target="tpu_custom_call" | custom-call | flops 14495514624 | bytes 18874368 | tf_op jit(solution)/shard_map/pallas_call | solution.py:422
  51.1 1.3 %slice_bitcast_fusion = (f32[128]{0:T(128)}, f32[128]{0:T(128)}, f32[128]{0:T(128)}) fusion(f32[4,128]{1,0:T(4,128)} %shard_map.84), kind=kLoop, calls=%fused_computation | loop fusion | bytes 3072 | tf_op jit(solution)/shard_map/squeeze | solution.py:471
  52.4 1.2 %slice.15 = f32[1,1]{1,0:T(1,128)} slice(f32[4,128]{1,0:T(4,128)} %shard_map.84), slice={[3:4], [0:1]} | slice | bytes 8 | tf_op jit(solution)/shard_map/slice | solution.py:471

commit v5 on v4

--- a/solution.py
+++ b/solution.py
@@ -29,7 +29,7 @@
     nreq, nvoc, hidden_in, gain_in, targets_in, bounds_in, head, out,
     hidden, gain, targets, bounds, rows, weights, first, second, top, total, weighted, picked, group,
     meta, stats, stats_out, ent, ent_sum,
-    in_sem, head_sem, rows_rx, down_tx, up_tx, side_tx, extra_tx, meta_rx, meta_tx, stats_rx, stats_tx,
+    in_sem, head_sem, rows_rx, down_tx, up_tx, side_tx, meta_rx, meta_tx, stats_rx, stats_tx,
     ent_rx, ent_tx, sum_rx, sum_tx,
 ):
     nz = nvoc // SIDE
@@ -95,20 +95,14 @@
             recv_sem=rows_rx.at[block, half], device_id={"voc": target},
         )
 
-    def send_down(place, half):
-        return send_rows(at(place, x), half, at(z - 1, x), down_tx.at[place, half])
-
-    def send_up(place, half):
-        return send_rows(at(place, x), half, at(z + 1, x), up_tx.at[place, half])
+    def send_down(far, half):
+        return send_rows(me, half, at(z - far, x), down_tx.at[far, half])
+
+    def send_up(far, half):
+        return send_rows(me, half, at(z + far, x), up_tx.at[far, half])
 
     def send_side(place, half):
         return send_rows(at(place, x), half, partner, side_tx.at[place, half])
-
-    def extra_up():
-        return send_rows(at(0, SIDE - 1 - x), 1, at(z + 1, x), extra_tx.at[0])
-
-    def extra_down():
-        return send_rows(at(nz - 1, SIDE - 1 - x), 1, at(z - 1, x), extra_tx.at[1])
 
     def wait_rows(block, half):
         send_rows(block, half, partner, side_tx.at[0, 0]).wait_recv()
@@ -119,16 +113,12 @@
             recv_sem=meta_rx.at[me], device_id={"voc": lax.rem(me + i, nvoc)},
         )
 
-    for half in range(2):
-        @pl.when(z > 0)
-        def _():
-            send_down(z, half).start()
-
-        @pl.when(z < nz - 1)
-        def _():
-            send_up(z, half).start()
-
-        send_side(z, half).start()
+    for far in range(1, nz):
+        for half in range(2):
+            pl.when(z >= far)(lambda: send_down(far, half).start())
+            pl.when(z + far < nz)(lambda: send_up(far, half).start())
+            if far == 1:
+                send_side(z, half).start()
     for i in range(1, nvoc):
         send_meta(i).start()
 
@@ -197,49 +187,16 @@
         @pl.when(z - t >= 0)
         def _():
             wait_rows(at(z - t, x), half)
-
-            @pl.when(z < nz - 1)
-            def _():
-                send_up(z - t, half).start()
-
-            @pl.when((half == 0) | (z - t > 0))
-            def _():
-                send_side(z - t, half).start()
+            send_side(z - t, half).start()
 
         @pl.when(z + t < nz)
         def _():
             wait_rows(at(z + t, x), half)
-
-            @pl.when(z > 0)
-            def _():
-                send_down(z + t, half).start()
-
-            @pl.when((half == 0) | (z + t < nz - 1))
-            def _():
-                send_side(z + t, half).start()
-
-        gap = t - 1
-        due = (t == 1) if half == 1 else (t > 1)
-
-        @pl.when(due & (z == gap))
-        def _():
-            wait_rows(at(0, SIDE - 1 - x), 1)
-            extra_up().start()
-
-        @pl.when(due & (nz - 1 - z == gap))
-        def _():
-            wait_rows(at(nz - 1, SIDE - 1 - x), 1)
-            extra_down().start()
+            send_side(z + t, half).start()
 
     def wait_across(place):
-        block = at(place, SIDE - 1 - x)
-        wait_rows(block, 0)
-        inner = (place > 0) & (place < nz - 1)
-        opposite = (place - z == nz - 1) | (z - place == nz - 1)
-
-        @pl.when(inner | opposite)
-        def _():
-            wait_rows(block, 1)
+        for half in range(2):
+            wait_rows(at(place, SIDE - 1 - x), half)
 
     def work(blocks, fresh, middle=None):
         steps = chunks // 2 - 1
@@ -391,16 +348,12 @@
     mean = jnp.broadcast_to(summed[0:1] / summed[1:2], (1, slots))
     out[...] = jnp.concatenate([row_logprob, row_entropy, row_picked, mean], axis=0)
 
-    for place in range(nz):
-        for half in range(2):
-            if half == 0 or 0 < place < nz - 1:
-                send_side(place, half).wait_send()
-            else:
-                pl.when(z == place)(lambda: send_side(place, half).wait_send())
-            pl.when((z > 0) & (z <= place))(lambda: send_down(place, half).wait_send())
-            pl.when((z < nz - 1) & (z >= place))(lambda: send_up(place, half).wait_send())
-    pl.when(z < nz - 1)(lambda: extra_up().wait_send())
-    pl.when(z > 0)(lambda: extra_down().wait_send())
+    for half in range(2):
+        for place in range(nz):
+            send_side(place, half).wait_send()
+        for far in range(1, nz):
+            pl.when(z >= far)(lambda: send_down(far, half).wait_send())
+            pl.when(z + far < nz)(lambda: send_up(far, half).wait_send())
 
     for i in range(1, nvoc):
         send_meta(i).wait_send()
@@ -449,7 +402,6 @@
             dma((nz, 2)),
             dma((nz, 2)),
             dma((nz, 2)),
-            dma((2,)),
             dma((nvoc,)),
             dma((nvoc,)),
             dma((nvoc,)),

time: 53.8 us -> 67.8 us (1.26)
  Pallas kernels: 50.4 us -> 64.5 us
    pallas_call x1, Pallas kernels: 50.4 us -> 64.5 us  [shards(): pl.pallas_call(functools.partial(kernel, nreq, nvoc), out_shape=jax.Shape...]
where the time goes in v5:
time: 67.8 us; the launch traced here: 67.6 us
  Pallas kernels  64.5 us (95%)
  local copies, waits for them, and re-layouts  2.49 us (4%)
    pallas_call x1, Pallas kernels, shards(): pl.pallas_call(functools.partial(kernel, nreq, nvoc), out_shape=jax.Shape...  64.5 us

profile of v5, /device:TPU:0, one launch (start us, length us, event | category | flops | bytes accessed | tf_op | source)
XLA Modules:
  0.0 67.6 jit_solution(11387037451161357985)
XLA Ops:
  0.6 64.5 %shard_map.84 = f32[4,128]{1,0:T(4,128)} custom-call(bf16[128,1536]{1,0:T(8,128)(2,1)} %hidden_in.1, f32[12,128]{1,0:T(8,128)} %bitcast.9, s32[1,128]{1,0:T(1,128)} %bitcast.10, s32[1,2]{1,0:T(1,128)} %bounds_in.1, bf16[1536,6144]{1,0:T(8,128)(2,1)} %head.1), custom_call_target="tpu_custom_call" | custom-call | flops 14495514624 | bytes 18874368 | tf_op jit(solution)/shard_map/pallas_call | solution.py:375
  65.1 1.3 %slice_bitcast_fusion = (f32[128]{0:T(128)}, f32[128]{0:T(128)}, f32[128]{0:T(128)}) fusion(f32[4,128]{1,0:T(4,128)} %shard_map.84), kind=kLoop, calls=%fused_computation | loop fusion | bytes 3072 | tf_op jit(solution)/shard_map/squeeze | solution.py:423
  66.4 1.2 %slice.15 = f32[1,1]{1,0:T(1,128)} slice(f32[4,128]{1,0:T(4,128)} %shard_map.84), slice={[3:4], [0:1]} | slice | bytes 8 | tf_op jit(solution)/shard_map/slice | solution.py:423
